TPU v7x, 1024 devices: a whole 8x8x8 slice. The times are simulated.
1024 devices in a mesh: ia: 4 (over x_lo, core), ja: 8 (over y), ka: 32 (over z, x_hi).
Axes of the slice: x: 8 (x_hi: 4, x_lo: 2; x = x_hi * 2 + x_lo), y: 8, z: 8, core: 2. Of those that a mesh axis runs over, the one named last changes fastest.
Arguments:
- tensor: float32 [16, 2048, 8192], P('ia', 'ja', 'ka'), may hold values from -6 to 6
- factor_a: float32 [16, 64], replicated, may hold values from -0.03125 to 0.03125
- factor_b: float32 [2048, 64], P(('ja', 'ia', 'ka')), may hold values from -60 to 60
- factor_c: float32 [8192, 64], P(('ka', 'ia', 'ja')), may hold values from -60 to 60
Outputs:
- grad_b: float32 [2048, 64], P(('ja', 'ia', 'ka'))
- grad_c: float32 [8192, 64], P(('ka', 'ia', 'ja'))
All inputs are finite; a program needn't handle non-finite values.
Results may differ from a plain program's by a relative error of at most 0.0003.
Values sent between devices are 32-bit elements; how exact they have to be, the bound alone decides.
No kernel may reach another device: no remote copies, remote signals or barrier semaphores. Data moves between devices by JAX's collectives and lax.ppermute only.
A program may use at most 32 MiB of HBM per device.

v0:
```python
import jax
import jax.numpy as jnp
from jax import lax
from jax.sharding import PartitionSpec as P


def gram_matrix(matrix):
    return jnp.dot(
        matrix.T, matrix, precision=lax.Precision.HIGHEST, preferred_element_type=jnp.float32
    )


def per_device(tensor, factor_a, factor_b, factor_c):
    depth_rows, middle_rows, inner_rows = tensor.shape
    rank_width = factor_a.shape[1]
    first_offset = lax.axis_index("ia") * depth_rows
    local_a = lax.dynamic_slice_in_dim(factor_a, first_offset, depth_rows, 0)
    shard_rows = lax.all_gather(factor_c, ("ia", "ja"), axis=0, tiled=True)
    count = shard_rows.shape[0]
    block = tensor
    inner = jnp.dot(
        block.reshape(depth_rows * middle_rows, count),
        shard_rows,
        precision=lax.Precision.HIGHEST,
        preferred_element_type=jnp.float32,
    )
    inner = inner.reshape(depth_rows, middle_rows, rank_width)
    second_terms = jnp.einsum("ijr,ir->jr", inner, local_a, precision=lax.Precision.HIGHEST)
    shard_rows = lax.all_gather(factor_b, ("ia", "ka"), axis=0, tiled=True)
    count = shard_rows.shape[0]
    block = tensor
    weights = (local_a[:, None, :] * shard_rows[None, :, :]).reshape(depth_rows * count, rank_width)
    flat = block.reshape(depth_rows * count, inner_rows)
    third_terms = lax.dot_general(
        flat,
        weights,
        (((0,), (0,)), ((), ())),
        precision=lax.Precision.HIGHEST,
        preferred_element_type=jnp.float32,
    )
    gram_b, gram_c = lax.psum((gram_matrix(factor_b), gram_matrix(factor_c)), ("ia", "ja", "ka"))
    owned_second = lax.psum_scatter(second_terms, ("ia", "ka"), scatter_dimension=0, tiled=True)
    owned_third = lax.psum_scatter(third_terms, ("ia", "ja"), scatter_dimension=0, tiled=True)
    gram_a = gram_matrix(factor_a)
    grad_b = (
        jnp.dot(
            factor_b,
            gram_a * gram_c,
            precision=lax.Precision.HIGHEST,
            preferred_element_type=jnp.float32,
        )
        - owned_second
    )
    grad_c = (
        jnp.dot(
            factor_c,
            gram_a * gram_b,
            precision=lax.Precision.HIGHEST,
            preferred_element_type=jnp.float32,
        )
        - owned_third
    )
    return (grad_b, grad_c)


def solution(mesh):
    placed = (P("ia", "ja", "ka"), P(), P(("ja", "ia", "ka"), None), P(("ka", "ia", "ja"), None))
    return jax.shard_map(
        per_device,
        mesh=mesh,
        in_specs=placed,
        out_specs=(P(("ja", "ia", "ka"), None), P(("ka", "ia", "ja"), None)),
        check_vma=False,
    )
```

profile of v0, /device:TPU:1, one launch (start us, length us, event | category | flops | bytes accessed | tf_op | source)
XLA Modules:
  0.0 611.9 jit_solution(14633281106423154036)
XLA Ops:
  7.2 0.0 copy-start
  7.2 0.0 all-reduce.6.cloned.1.call-start
  7.2 0.0 copy-start.1
  7.2 0.8 copy-done.1
  8.0 0.0 copy-start.2
  8.0 61.9 %all_gather.6 = f32[256,64]{1,0:T(8,128)S(1)} all-gather(f32[8,64]{1,0:T(8,128)S(1)} %copy-done.1), channel_id=1, replica_groups=mesh['ia'=4,'ja'=8,'ka'=32] {'ia','ja'}, dimensions={0}, use_global_device_ids=true | all-gather | bytes 67584 | tf_op jit(solution)/shard_map/all_gather | solution.py:18
  69.9 0.0 copy-done.2
  69.9 0.0 copy-done
  69.9 1.6 fusion.1
  71.6 0.0 all-reduce.6.cloned.1.call-update
  71.6 0.0 all-reduce.8.cloned.1.call-start
  71.7 0.0 copy-start.3
  71.7 0.7 copy-done.3
  72.4 287.8 %all-gather = f32[128,2,64]{2,1,0:T(2,128)S(1)} all-gather(f32[1,2,64]{2,1,0:T(2,128)S(1)} %bitcast.40), channel_id=1, replica_groups=mesh['ia'=4,'ja'=8,'ka'=32] {'ia','ka'}, dimensions={0}, use_global_device_ids=true | all-gather | bytes 66048 | tf_op jit(solution)/shard_map/all_gather | solution.py:29
  360.1 0.1 copy.8
  360.2 0.7 convolution_bitcast_fusion.1
  360.9 0.8 copy.9
  361.7 0.0 all-reduce.8.cloned.1.call-update
  361.7 0.2 fusion.11
  362.0 0.2 fusion.12
  362.2 0.2 fusion.10
  362.4 1.3 dynamic-slice.2
  363.7 1.3 dynamic-slice
  365.0 134.7 %all-reduce.2 = (f32[64,64]{1,0:T(8,128)S(1)}, f32[64,64]{1,0:T(8,128)S(1)}) all-reduce(f32[64,64]{1,0:T(8,128)S(1)} %fusion.11, f32[64,64]{1,0:T(8,128)S(1)} %fusion.12), channel_id=1, replica_groups=mesh['ia'=4,'ja'=8,'ka'=32] {'ia','ja','ka'}, use_global_device_ids=true, to_apply=%region_0.0 | all-reduce | flops 8192 | bytes 65536 | tf_op jit(solution)/shard_map/psum | solution.py:41
  501.0 0.0 all-reduce.6.cloned.1.call-done
  501.0 1.4 fusion.3
  502.4 101.3 %all-reduce.8.cloned.1.call-done = f32[256,64]{1,0:T(8,128)} async-done(((f32[256,64]{1,0:T(8,128)}), f32[256,64]{1,0:T(8,128)}) %all-reduce.8.cloned.1.call-update) | async-done | bytes 65552
  603.7 1.4 fusion.2
  (2 shorter events, 0.0 us)
Async XLA Ops:
  7.2 62.8 %copy-start = (f32[4,256,256]{2,1,0:T(8,128)S(1)}, f32[4,256,256]{2,1,0:T(8,128)}, u32[]{:S(2)}) copy-start(f32[4,256,256]{2,1,0:T(8,128)} %param.4) | copy-start | bytes 3145732
  7.2 493.8 %all-reduce.6.cloned.1.call-start = ((), (), s32[]{:S(2)}) async-start(), calls=%async_computation | async-start | bytes 262144
  7.2 0.8 copy-start.1
  8.0 61.9 %copy-start.2 = (f32[16,64]{1,0:T(8,128)S(1)}, f32[16,64]{1,0:T(8,128)}, u32[]{:S(2)}) copy-start(f32[16,64]{1,0:T(8,128)} %param.5) | copy-start | bytes 12292
  71.6 532.1 %all-reduce.8.cloned.1.call-start = ((), (), s32[]{:S(2)}) async-start(), calls=%async_computation.1 | async-start | bytes 262144
  71.7 0.7 copy-start.3
Sparse Core Ops, SparseCore 0:
  71.7 200.1 all-reduce.5
  361.8 241.7 all-reduce.7
where the time goes:
time: 612 us
  blocking collectives  484 us (79%)
  waiting for transfers between devices  101 us (17%)
  between operations  15.4 us (3%)
    all_gather x1, blocking collectives, per_device(): shard_rows = lax.all_gather(factor_b, ('ia', 'ka'), axis=0, tiled=True)  288 us
    psum x1, blocking collectives, per_device(): lax.psum((gram_matrix(factor_b), gram_matrix(factor_c)), ('ia', 'ja', 'ka'))  135 us
    unnamed x4, waiting for transfers between devices  101 us
    all_gather x1, blocking collectives, per_device(): shard_rows = lax.all_gather(factor_c, ('ia', 'ja'), axis=0, tiled=True)  61.9 us
  transfers between devices with their start and end apart: 2, of which 1 were waited for; matrix products, arithmetic and copies ran while one was open for 1% of the time, Pallas kernels for 0%

commit v1 on v0

v1 whole, which is shorter than its diff:
```python
import jax
import jax.numpy as jnp
from jax import lax
from jax.experimental import pallas as pl
from jax.experimental.pallas import tpu as pltpu
from jax.sharding import PartitionSpec as P

F32 = jnp.float32
BF16 = jnp.bfloat16
VMEM = pl.BlockSpec(memory_space=pltpu.VMEM)

NI, NJ, NK = 4, 8, 32
NP = NI * NJ
R = 64
ROWS = 256
M1, M2, M3 = 5, 9, 6


def coords():
    return lax.axis_index("ia"), lax.axis_index("ja")


def split(x):
    hi = x.astype(BF16)
    return hi, (x - hi.astype(F32)).astype(BF16)


def dot(x, y):
    return jnp.dot(x, y, preferred_element_type=F32)


def dot_exact(x, y, dims):
    return lax.dot_general(
        x, y, (dims, ((), ())), precision=lax.Precision.HIGHEST, preferred_element_type=F32
    )


def pack_kernel(b_ref, c_ref, out_ref):
    for q in range(4):
        row = jnp.concatenate([c_ref[q : q + 1, :], c_ref[q + 4 : q + 5, :]], axis=1)
        out_ref[pl.ds(q, NP, stride=M1), :] = jnp.broadcast_to(row, (NP, 2 * R))
    row = jnp.concatenate([b_ref[0:1, :], b_ref[1:2, :]], axis=1)
    out_ref[pl.ds(4, NP, stride=M1), :] = jnp.broadcast_to(row, (NP, 2 * R))


def second_kernel(t_ref, a_ref, r1_ref, out_ref, c_ref, sec_ref, gram_ref):
    ia, ja = coords()
    for q in range(4):
        rows = r1_ref[pl.ds(q, NP, stride=M1), :]
        c_ref[pl.ds(q, NP, stride=8), :] = rows[:, :R]
        c_ref[pl.ds(q + 4, NP, stride=8), :] = rows[:, R:]
    c = c_ref[...]
    second = None
    for i in range(NI):
        w_hi, w_lo = split(c * a_ref[pl.ds(NI * ia + i, 1), :])
        t_hi, t_lo = split(t_ref[i])
        part = dot(t_hi, w_hi) + (dot(t_hi, w_lo) + dot(t_lo, w_hi))
        second = part if second is None else second + part
    sec_ref[...] = second
    gram_ref[...] = dot_exact(c, c, ((0,), (0,)))
    p = ia * NJ + ja
    for i in range(NI):
        row = r1_ref[pl.ds((i * NJ + ja) * M1 + 4, 1), :]
        out_ref[pl.ds(i, NK, stride=M2), :] = jnp.broadcast_to(row, (NK, 2 * R))
        even = sec_ref[pl.ds(i * 2 * NK, NK, stride=2), :]
        odd = sec_ref[pl.ds(i * 2 * NK + 1, NK, stride=2), :]
        out_ref[pl.ds(4 + i, NK, stride=M2), :] = jnp.concatenate([even, odd], axis=1)
    row = jnp.concatenate([gram_ref[pl.ds(2 * p, 1), :], gram_ref[pl.ds(2 * p + 1, 1), :]], axis=1)
    out_ref[pl.ds(8, NK, stride=M2), :] = jnp.broadcast_to(row, (NK, 2 * R))


def third_kernel(t_ref, a_ref, c_ref, r2_ref, out_ref, b_ref, third_ref):
    ia, _ = coords()
    for i in range(NI):
        rows = r2_ref[pl.ds(i, NK, stride=M2), :]
        b_ref[pl.ds(i * 2 * NK, NK, stride=2), :] = rows[:, :R]
        b_ref[pl.ds(i * 2 * NK + 1, NK, stride=2), :] = rows[:, R:]
    b = b_ref[...]
    a = a_ref[pl.ds(NI * ia, NI), :]
    third = None
    for h in range(NI // 2):
        pair = jnp.concatenate([b * a[2 * h : 2 * h + 1, :], b * a[2 * h + 1 : 2 * h + 2, :]], axis=1)
        w_hi, w_lo = split(pair.T)
        for e in range(2):
            t_hi, t_lo = split(t_ref[2 * h + e])
            x_hi, x_lo = w_hi[e * R : (e + 1) * R, :], w_lo[e * R : (e + 1) * R, :]
            part = dot(x_hi, t_hi) + (dot(x_lo, t_hi) + dot(x_hi, t_lo))
            third = part if third is None else third + part
    gram_b = dot_exact(b, b, ((0,), (0,)))
    gram_a = dot_exact(a, a, ((0,), (0,)))
    third_ref[...] = dot_exact(c_ref[...], gram_a * gram_b, ((1,), (0,))) - third.T
    for q in range(4):
        left = third_ref[pl.ds(q, NP, stride=8), :]
        right = third_ref[pl.ds(q + 4, NP, stride=8), :]
        out_ref[pl.ds(q, NP, stride=M3), :] = jnp.concatenate([left, right], axis=1)
    for i in range(NI):
        row = jnp.sum(r2_ref[pl.ds(4 + i, NK, stride=M2), :], axis=0, keepdims=True)
        out_ref[pl.ds(i * NJ * M3 + 4, NJ, stride=M3), :] = jnp.broadcast_to(row, (NJ, 2 * R))
    row = jnp.sum(r2_ref[pl.ds(8, NK, stride=M2), :], axis=0, keepdims=True)
    out_ref[pl.ds(5, NP, stride=M3), :] = jnp.broadcast_to(row, (NP, 2 * R))


def final_kernel(a_ref, b_ref, r3_ref, gb_ref, gc_ref, gram_ref):
    _, ja = coords()
    for q in range(4):
        row = jnp.sum(r3_ref[pl.ds(q, NP, stride=M3), :], axis=0, keepdims=True)
        gc_ref[q : q + 1, :] = row[:, :R]
        gc_ref[q + 4 : q + 5, :] = row[:, R:]
    rows = r3_ref[pl.ds(5, NP, stride=M3), :]
    gram_ref[pl.ds(0, NP, stride=2), :] = rows[:, :R]
    gram_ref[pl.ds(1, NP, stride=2), :] = rows[:, R:]
    a = a_ref[...]
    gram_a = dot_exact(a, a, ((0,), (0,)))
    b = jnp.concatenate([b_ref[...], jnp.zeros((6, R), F32)], axis=0)
    gb = dot_exact(b, gram_a * gram_ref[...], ((1,), (0,)))
    row = r3_ref[pl.ds(ja * M3 + 4, 1), :]
    for i in range(1, NI):
        row = row + r3_ref[pl.ds((i * NJ + ja) * M3 + 4, 1), :]
    gb_ref[0:1, :] = gb[0:1, :] - row[:, :R]
    gb_ref[1:2, :] = gb[1:2, :] - row[:, R:]


def call(kernel, outs, operands, scratch=()):
    return pl.pallas_call(
        kernel,
        out_shape=[jax.ShapeDtypeStruct(shape, F32) for shape in outs],
        in_specs=[VMEM] * len(operands),
        out_specs=[VMEM] * len(outs),
        scratch_shapes=[pltpu.VMEM(shape, F32) for shape in scratch],
        compiler_params=pltpu.CompilerParams(vmem_limit_bytes=16 * 1024 * 1024),
    )(*operands)


def exchange(x, axes, rows):
    peers = x.shape[0] // rows
    x = x.reshape(peers, rows, 1, 2 * R)
    x = lax.all_to_all(x, axes, 0, 0)
    return x.reshape(peers * rows, 2 * R)


def per_device(tensor, factor_a, factor_b, factor_c):
    (s1,) = call(pack_kernel, [(NP * M1, 2 * R)], (factor_b, factor_c))
    r1 = exchange(s1, ("ia", "ja"), M1)
    s2, c = call(
        second_kernel,
        [(NK * M2, 2 * R), (ROWS, R)],
        (tensor, factor_a, r1),
        [(ROWS, R), (R, R)],
    )
    r2 = exchange(s2, "ka", M2)
    (s3,) = call(
        third_kernel,
        [(NP * M3, 2 * R)],
        (tensor, factor_a, c, r2),
        [(ROWS, R), (ROWS, R)],
    )
    r3 = exchange(s3, ("ia", "ja"), M3)
    gb, gc = call(final_kernel, [(2, R), (8, R)], (factor_a, factor_b, r3), [(R, R)])
    return gb, gc


def solution(mesh):
    placed = (P("ia", "ja", "ka"), P(), P(("ja", "ia", "ka"), None), P(("ka", "ia", "ja"), None))
    return jax.shard_map(
        per_device,
        mesh=mesh,
        in_specs=placed,
        out_specs=(P(("ja", "ia", "ka"), None), P(("ka", "ia", "ja"), None)),
        check_vma=False,
    )
```

time: 612 us -> 70.8 us (0.12)
  blocking collectives: 484 us -> 63.5 us
  waiting for transfers between devices: 101 us -> 0 us
  between operations: 15.4 us -> 0.65 us
    all_gather x2 -> x0, blocking collectives: 350 us -> none  [the longest x1 288 us: per_device(): shard_rows = lax.all_gather(factor_b, ('ia', 'ka'), axis=0, tiled=True)]
    psum x1 -> x0, blocking collectives: 135 us -> none  [per_device(): lax.psum((gram_matrix(factor_b), gram_matrix(factor_c)), ('ia', 'ja', 'ka'))]
    unnamed x4 -> x0, waiting for transfers between devices: 101 us -> none
    all_to_all x0 -> x3, blocking collectives: none -> 63.5 us  [exchange(): x = lax.all_to_all(x, axes, 0, 0)]
  transfers between devices with their start and end apart: 2 -> 0, of which waited for: 1 -> 0; matrix products, arithmetic and copies ran while one was open for 1% -> 0% of each run, Pallas kernels for 0% -> 0%
where the time goes in v1:
time: 70.8 us; the launch traced here: 70.5 us
  blocking collectives  63.5 us (90%)
  local copies, waits for them, and re-layouts  3.27 us (5%)
  Pallas kernels  3.02 us (4%)
    all_to_all x3, blocking collectives, exchange(): x = lax.all_to_all(x, axes, 0, 0)  63.5 us
    unnamed x10, local copies, waits for them, and re-layouts  3.27 us
    pallas_call x4, Pallas kernels, call(): pl.pallas_call(kernel, out_shape=[jax.ShapeDtypeStruct(shape, F32) for sh...  3.02 us

profile of v1, /device:TPU:1, one launch (start us, length us, event | category | flops | bytes accessed | tf_op | source)
XLA Modules:
  0.0 70.5 jit_solution(9248449826781106160)
XLA Ops:
  0.6 0.0 copy-start.2
  0.6 0.7 copy-done.2
  1.3 0.0 copy-start.4
  1.3 0.7 copy-done.4
  2.0 0.1 shard_map.59
  2.1 0.0 copy-start.1
  2.1 25.3 %all_to_all.15 = f32[32,5,1,128]{3,2,1,0:T(1,128)S(1)} all-to-all(f32[32,5,1,128]{3,2,1,0:T(1,128)S(1)} %bitcast.10), channel_id=1, replica_groups=mesh['ia'=4,'ja'=8,'ka'=32] {'ia','ja'}, dimensions={0} | all-to-all | bytes 163840 | tf_op jit(solution)/shard_map/all_to_all | solution.py:137
  27.4 0.0 copy-done.1
  27.4 0.0 copy-start
  27.4 1.2 %copy-done = f32[4,256,256]{2,1,0:T(8,128)S(1)} copy-done((f32[4,256,256]{2,1,0:T(8,128)S(1)}, f32[4,256,256]{2,1,0:T(8,128)}, u32[]{:S(2)}) %copy-start) | copy-done | bytes 1048600
  28.6 0.8 %shard_map.60 = (f32[288,128]{1,0:T(8,128)S(1)}, f32[256,64]{1,0:T(8,128)S(1)}) custom-call(f32[4,256,256]{2,1,0:T(8,128)S(1)} %copy-done, f32[16,64]{1,0:T(8,128)S(1)} %copy-done.1, f32[160,128]{1,0:T(8,128)S(1)} %bitcast.9), custom_call_target="tpu_custom_call" | custom-call | tf_op jit(solution)/shard_map/pallas_call | solution.py:124
  29.4 25.0 %all_to_all.16 = f32[32,9,1,128]{3,2,1,0:T(1,128)S(1)} all-to-all(f32[32,9,1,128]{3,2,1,0:T(1,128)S(1)} %bitcast.11), channel_id=1, replica_groups=mesh['ia'=4,'ja'=8,'ka'=32] {'ka'}, dimensions={0} | all-to-all | bytes 294912 | tf_op jit(solution)/shard_map/all_to_all | solution.py:137
  54.4 1.2 %shard_map.61 = f32[192,128]{1,0:T(8,128)S(1)} custom-call(f32[4,256,256]{2,1,0:T(8,128)S(1)} %copy-done, f32[16,64]{1,0:T(8,128)S(1)} %copy-done.1, f32[256,64]{1,0:T(8,128)S(1)} %get-tuple-element.4.c_ref, f32[288,128]{1,0:T(8,128)S(1)} %bitcast.6), custom_call_target="tpu_custom_call" | custom-call | tf_op jit(solution)/shard_map/pallas_call | solution.py:124
  55.5 13.3 %all_to_all.17 = f32[32,6,1,128]{3,2,1,0:T(1,128)S(1)} all-to-all(f32[32,6,1,128]{3,2,1,0:T(1,128)S(1)} %bitcast.8), channel_id=1, replica_groups=mesh['ia'=4,'ja'=8,'ka'=32] {'ia','ja'}, dimensions={0} | all-to-all | bytes 196608 | tf_op jit(solution)/shard_map/all_to_all | solution.py:137
  68.8 0.0 copy-start.3
  68.8 0.7 copy-done.3
  69.5 1.0 %shard_map.62 = (f32[2,64]{1,0:T(2,128)}, f32[8,64]{1,0:T(8,128)}) custom-call(f32[16,64]{1,0:T(8,128)S(1)} %copy-done.1, f32[2,64]{1,0:T(2,128)S(1)} %copy-done.3, f32[192,128]{1,0:T(8,128)S(1)} %bitcast.7), custom_call_target="tpu_custom_call" | custom-call | tf_op jit(solution)/shard_map/pallas_call | solution.py:124
Async XLA Ops:
  0.6 0.7 copy-start.2
  1.3 0.7 copy-start.4
  2.1 25.3 %copy-start.1 = (f32[16,64]{1,0:T(8,128)S(1)}, f32[16,64]{1,0:T(8,128)}, u32[]{:S(2)}) copy-start(f32[16,64]{1,0:T(8,128)} %a_ref.5) | copy-start | bytes 12292
  27.4 1.2 %copy-start = (f32[4,256,256]{2,1,0:T(8,128)S(1)}, f32[4,256,256]{2,1,0:T(8,128)}, u32[]{:S(2)}) copy-start(f32[4,256,256]{2,1,0:T(8,128)} %t_ref.3) | copy-start | bytes 3145732
  68.8 0.7 copy-start.3

commit v2 on v1

v2 whole, which is shorter than its diff:
```python
import jax
import jax.numpy as jnp
from jax import lax
from jax.experimental import pallas as pl
from jax.experimental.pallas import tpu as pltpu
from jax.sharding import PartitionSpec as P

F32 = jnp.float32
BF16 = jnp.bfloat16
VMEM = pl.BlockSpec(memory_space=pltpu.VMEM)
HBM = pl.BlockSpec(memory_space=pltpu.HBM)

NI, NJ, NK = 4, 8, 32
NP = NI * NJ
R = 64
ROWS = 256
M1, M2, M3 = 5, 9, 5


def coords():
    return lax.axis_index("ia"), lax.axis_index("ja")


def split(x):
    hi = x.astype(BF16)
    return hi, (x - hi.astype(F32)).astype(BF16)


def dot(x, y):
    return jnp.dot(x, y, preferred_element_type=F32)


def dot_exact(x, y, dims):
    return lax.dot_general(
        x, y, (dims, ((), ())), precision=lax.Precision.HIGHEST, preferred_element_type=F32
    )


def fetch(source, target, sem):
    copy = pltpu.make_async_copy(source, target, sem)
    copy.start()
    return copy


def pack_kernel(b_hbm, c_hbm, t_hbm, out_ref, t_ref, b_ref, c_ref, sems):
    copies = [fetch(b_hbm, b_ref, sems.at[0]), fetch(c_hbm, c_ref, sems.at[1])]
    block = fetch(t_hbm, t_ref, sems.at[2])
    for copy in copies:
        copy.wait()
    for q in range(4):
        row = jnp.concatenate([c_ref[q : q + 1, :], c_ref[q + 4 : q + 5, :]], axis=1)
        out_ref[pl.ds(q, NP, stride=M1), :] = jnp.broadcast_to(row, (NP, 2 * R))
    row = jnp.concatenate([b_ref[0:1, :], b_ref[1:2, :]], axis=1)
    out_ref[pl.ds(4, NP, stride=M1), :] = jnp.broadcast_to(row, (NP, 2 * R))
    block.wait()


def second_kernel(t_ref, a_ref, r1_ref, out_ref, c_ref, sec_ref, gram_ref):
    ia, ja = coords()
    p = ia * NJ + ja
    for q in range(4):
        rows = r1_ref[pl.ds(q, NP, stride=M1), :]
        c_ref[pl.ds(q, NP, stride=8), :] = rows[:, :R]
        c_ref[pl.ds(q + 4, NP, stride=8), :] = rows[:, R:]
    c = c_ref[...]
    a = a_ref[...]
    gram_a = dot_exact(a, a, ((0,), (0,)))
    gram_ref[...] = gram_a * dot_exact(c, c, ((0,), (0,)))
    row = jnp.concatenate([gram_ref[pl.ds(2 * p, 1), :], gram_ref[pl.ds(2 * p + 1, 1), :]], axis=1)
    out_ref[pl.ds(8, NK, stride=M2), :] = jnp.broadcast_to(row, (NK, 2 * R))
    for i in range(NI):
        row = r1_ref[pl.ds((i * NJ + ja) * M1 + 4, 1), :]
        out_ref[pl.ds(i, NK, stride=M2), :] = jnp.broadcast_to(row, (NK, 2 * R))
    weights = [split(c * a_ref[pl.ds(NI * ia + i, 1), :]) for i in range(NI)]
    second = None
    for i in range(NI):
        w_hi, w_lo = weights[i]
        t_hi, t_lo = split(t_ref[i])
        part = dot(t_hi, w_hi) + (dot(t_hi, w_lo) + dot(t_lo, w_hi))
        second = part if second is None else second + part
    sec_ref[...] = second
    for i in range(NI):
        even = sec_ref[pl.ds(i * 2 * NK, NK, stride=2), :]
        odd = sec_ref[pl.ds(i * 2 * NK + 1, NK, stride=2), :]
        out_ref[pl.ds(4 + i, NK, stride=M2), :] = jnp.concatenate([even, odd], axis=1)


def third_kernel(t_ref, a_ref, c_ref, r1_ref, r2_ref, out_ref, b_ref, third_ref):
    ia, ja = coords()
    p = ia * NJ + ja
    for i in range(NI):
        rows = r2_ref[pl.ds(i, NK, stride=M2), :]
        b_ref[pl.ds(i * 2 * NK, NK, stride=2), :] = rows[:, :R]
        b_ref[pl.ds(i * 2 * NK + 1, NK, stride=2), :] = rows[:, R:]
    b = b_ref[...]
    a = a_ref[pl.ds(NI * ia, NI), :]
    gram_b = dot_exact(b, b, ((0,), (0,)))
    gram_a = dot_exact(a, a, ((0,), (0,)))
    row = jnp.sum(r2_ref[pl.ds(8, NK, stride=M2), :], axis=0, keepdims=True)
    place = lax.broadcasted_iota(jnp.int32, (R, R), 0)
    gram = jnp.where(place == 2 * p, row[:, :R], jnp.where(place == 2 * p + 1, row[:, R:], 0.0))
    rows = r1_ref[pl.ds(4, NP, stride=M1), :]
    grad_b = dot_exact(jnp.concatenate([rows[:, :R], rows[:, R:]], axis=0), gram, ((1,), (0,)))
    grad_b = jnp.concatenate([grad_b[:NP, :], grad_b[NP:, :]], axis=1)
    summed = jnp.concatenate(
        [
            jnp.broadcast_to(
                jnp.sum(r2_ref[pl.ds(4 + i, NK, stride=M2), :], axis=0, keepdims=True), (NJ, 2 * R)
            )
            for i in range(NI)
        ],
        axis=0,
    )
    peer = lax.broadcasted_iota(jnp.int32, (NP, 2 * R), 0)
    grad_b = grad_b - jnp.where(lax.rem(peer, NJ) == ja, summed, 0.0)
    out_ref[pl.ds(4, NP, stride=M3), :] = grad_b
    third = None
    for h in range(NI // 2):
        pair = jnp.concatenate([b * a[2 * h : 2 * h + 1, :], b * a[2 * h + 1 : 2 * h + 2, :]], axis=1)
        w_hi, w_lo = split(pair.T)
        for e in range(2):
            t_hi, t_lo = split(t_ref[2 * h + e])
            x_hi, x_lo = w_hi[e * R : (e + 1) * R, :], w_lo[e * R : (e + 1) * R, :]
            part = dot(x_hi, t_hi) + (dot(x_lo, t_hi) + dot(x_hi, t_lo))
            third = part if third is None else third + part
    third_ref[...] = dot_exact(c_ref[...], gram_a * gram_b, ((1,), (0,))) - third.T
    for q in range(4):
        left = third_ref[pl.ds(q, NP, stride=8), :]
        right = third_ref[pl.ds(q + 4, NP, stride=8), :]
        out_ref[pl.ds(q, NP, stride=M3), :] = jnp.concatenate([left, right], axis=1)


def final_kernel(r3_ref, gb_ref, gc_ref):
    for q in range(4):
        row = jnp.sum(r3_ref[pl.ds(q, NP, stride=M3), :], axis=0, keepdims=True)
        gc_ref[q : q + 1, :] = row[:, :R]
        gc_ref[q + 4 : q + 5, :] = row[:, R:]
    row = jnp.sum(r3_ref[pl.ds(4, NP, stride=M3), :], axis=0, keepdims=True)
    gb_ref[0:1, :] = row[:, :R]
    gb_ref[1:2, :] = row[:, R:]


def call(kernel, outs, operands, scratch=(), copies=0, in_hbm=0):
    scratch_shapes = [pltpu.VMEM(shape, F32) for shape in scratch]
    if copies:
        scratch_shapes.append(pltpu.SemaphoreType.DMA((copies,)))
    return pl.pallas_call(
        kernel,
        out_shape=[jax.ShapeDtypeStruct(shape, F32) for shape in outs],
        in_specs=[HBM] * in_hbm + [VMEM] * (len(operands) - in_hbm),
        out_specs=[VMEM] * len(outs),
        scratch_shapes=scratch_shapes,
        compiler_params=pltpu.CompilerParams(vmem_limit_bytes=16 * 1024 * 1024),
    )(*[pltpu.with_memory_space_constraint(x, pltpu.HBM) for x in operands[:in_hbm]], *operands[in_hbm:])


def exchange(x, axes, rows):
    peers = x.shape[0] // rows
    x = x.reshape(peers, rows, 1, 2 * R)
    x = lax.all_to_all(x, axes, 0, 0)
    return x.reshape(peers * rows, 2 * R)


def per_device(tensor, factor_a, factor_b, factor_c):
    s1, block = call(
        pack_kernel,
        [(NP * M1, 2 * R), tensor.shape],
        (factor_b, factor_c, tensor),
        [(2, R), (8, R)],
        copies=3,
        in_hbm=3,
    )
    r1 = exchange(s1, ("ia", "ja"), M1)
    s2, c = call(
        second_kernel,
        [(NK * M2, 2 * R), (ROWS, R)],
        (block, factor_a, r1),
        [(ROWS, R), (R, R)],
    )
    r2 = exchange(s2, "ka", M2)
    (s3,) = call(
        third_kernel,
        [(NP * M3, 2 * R)],
        (block, factor_a, c, r1, r2),
        [(ROWS, R), (ROWS, R)],
    )
    r3 = exchange(s3, ("ia", "ja"), M3)
    return tuple(call(final_kernel, [(2, R), (8, R)], (r3,)))


def solution(mesh):
    placed = (P("ia", "ja", "ka"), P(), P(("ja", "ia", "ka"), None), P(("ka", "ia", "ja"), None))
    return jax.shard_map(
        per_device,
        mesh=mesh,
        in_specs=placed,
        out_specs=(P(("ja", "ia", "ka"), None), P(("ka", "ia", "ja"), None)),
        check_vma=False,
    )
```

time: 70.8 us -> 68.1 us (0.962)
  local copies, waits for them, and re-layouts: 3.27 us -> 0.01 us
  Pallas kernels: 3.02 us -> 3.82 us
    unnamed x10 -> x2, local copies, waits for them, and re-layouts: 3.27 us -> 0.01 us
    pallas_call x4, Pallas kernels: 3.02 us -> 3.82 us  [call(): pl.pallas_call(kernel, out_shape=[jax.ShapeDtypeStruct(shape, F32) for sh...]
where the time goes in v2:
time: 68.1 us; the launch traced here: 67.8 us
  blocking collectives  63.4 us (93%)
  Pallas kernels  3.82 us (6%)
    all_to_all x3, blocking collectives, exchange(): x = lax.all_to_all(x, axes, 0, 0)  63.4 us
    pallas_call x4, Pallas kernels, call(): pl.pallas_call(kernel, out_shape=[jax.ShapeDtypeStruct(shape, F32) for sh...  3.82 us

profile of v2, /device:TPU:1, one launch (start us, length us, event | category | flops | bytes accessed | tf_op | source)
XLA Modules:
  0.0 67.8 jit_solution(1341575876041475553)
XLA Ops:
  0.6 1.3 %shard_map.59 = (f32[160,128]{1,0:T(8,128)S(1)}, f32[4,256,256]{2,1,0:T(8,128)S(1)}) custom-call(f32[2,64]{1,0:T(2,128)} %b_hbm.1, f32[8,64]{1,0:T(8,128)} %c_hbm.1, f32[4,256,256]{2,1,0:T(8,128)} %t_hbm.1), custom_call_target="tpu_custom_call" | custom-call | tf_op jit(solution)/shard_map/pallas_call | solution.py:147
  1.9 0.0 copy-start
  1.9 25.2 %all_to_all.15 = f32[32,5,1,128]{3,2,1,0:T(1,128)S(1)} all-to-all(f32[32,5,1,128]{3,2,1,0:T(1,128)S(1)} %bitcast.12), channel_id=1, replica_groups=mesh['ia'=4,'ja'=8,'ka'=32] {'ia','ja'}, dimensions={0} | all-to-all | bytes 163840 | tf_op jit(solution)/shard_map/all_to_all | solution.py:160
  27.1 0.0 copy-done
  27.1 0.9 %shard_map.60 = (f32[288,128]{1,0:T(8,128)S(1)}, f32[256,64]{1,0:T(8,128)S(1)}) custom-call(f32[4,256,256]{2,1,0:T(8,128)S(1)} %get-tuple-element.6.t_ref, f32[16,64]{1,0:T(8,128)S(1)} %copy-done, f32[160,128]{1,0:T(8,128)S(1)} %bitcast.6), custom_call_target="tpu_custom_call" | custom-call | tf_op jit(solution)/shard_map/pallas_call | solution.py:147
  28.0 25.0 %all_to_all.16 = f32[32,9,1,128]{3,2,1,0:T(1,128)S(1)} all-to-all(f32[32,9,1,128]{3,2,1,0:T(1,128)S(1)} %bitcast.11), channel_id=1, replica_groups=mesh['ia'=4,'ja'=8,'ka'=32] {'ka'}, dimensions={0} | all-to-all | bytes 294912 | tf_op jit(solution)/shard_map/all_to_all | solution.py:160
  52.9 1.0 %shard_map.61 = f32[160,128]{1,0:T(8,128)S(1)} custom-call(f32[4,256,256]{2,1,0:T(8,128)S(1)} %get-tuple-element.6.t_ref, f32[16,64]{1,0:T(8,128)S(1)} %copy-done, f32[256,64]{1,0:T(8,128)S(1)} %get-tuple-element.8.c_ref, f32[160,128]{1,0:T(8,128)S(1)} %bitcast.7, f32[288,128]{1,0:T(8,128)S(1)} %bitcast.8), custom_call_target="tpu_custom_call" | custom-call | tf_op jit(solution)/shard_map/pallas_call | solution.py:147
  53.9 13.2 %all_to_all.17 = f32[32,5,1,128]{3,2,1,0:T(1,128)S(1)} all-to-all(f32[32,5,1,128]{3,2,1,0:T(1,128)S(1)} %bitcast.9), channel_id=1, replica_groups=mesh['ia'=4,'ja'=8,'ka'=32] {'ia','ja'}, dimensions={0} | all-to-all | bytes 163840 | tf_op jit(solution)/shard_map/all_to_all | solution.py:160
  67.2 0.7 shard_map.62
Async XLA Ops:
  1.9 25.2 %copy-start = (f32[16,64]{1,0:T(8,128)S(1)}, f32[16,64]{1,0:T(8,128)}, u32[]{:S(2)}) copy-start(f32[16,64]{1,0:T(8,128)} %a_ref.3) | copy-start | bytes 12292

commit v3 on v2

v3 whole, which is shorter than its diff:
```python
import jax
import jax.numpy as jnp
from jax import lax
from jax.experimental import pallas as pl
from jax.experimental.pallas import tpu as pltpu
from jax.sharding import PartitionSpec as P

F32 = jnp.float32
BF16 = jnp.bfloat16
VMEM = pl.BlockSpec(memory_space=pltpu.VMEM)
HBM = pl.BlockSpec(memory_space=pltpu.HBM)

NI, NJ, NK = 4, 8, 32
NP = NI * NJ
R = 64
W = 2 * R
ROWS = 256
M1, M2, M3 = 5, 9, 5


def coords():
    return lax.axis_index("ia"), lax.axis_index("ja")


def rough(x):
    return x.astype(BF16).astype(F32)


def dot(x, y, dims=((1,), (0,))):
    return lax.dot_general(x, y, (dims, ((), ())), preferred_element_type=F32)


def dot_exact(x, y, dims):
    return lax.dot_general(
        x, y, (dims, ((), ())), precision=lax.Precision.HIGHEST, preferred_element_type=F32
    )


def left_half(x):
    return lax.broadcasted_iota(jnp.int32, x.shape, 1) < R


def join(x, y):
    return jnp.where(left_half(x), x, y)


def turned(x):
    return pltpu.roll(x, R, 1)


def twice(x):
    return x + turned(x)


def parts(x):
    return join(x, x - rough(x)).astype(BF16)


def split(x):
    hi = rough(x)
    return x.astype(BF16), (x - hi).astype(BF16)


def fetch(source, target, sem):
    copy = pltpu.make_async_copy(source, target, sem)
    copy.start()
    return copy


def pack_kernel(b_hbm, c_hbm, t_hbm, out_ref, t_ref, b_ref, c_ref, sems):
    block = fetch(t_hbm, t_ref, sems.at[2])
    copies = [fetch(b_hbm, b_ref, sems.at[0]), fetch(c_hbm, c_ref, sems.at[1])]
    for copy in copies:
        copy.wait()
    for q in range(4):
        row = jnp.concatenate([c_ref[q : q + 1, :], c_ref[q + 4 : q + 5, :]], axis=1)
        out_ref[pl.ds(q, NP, stride=M1), :] = jnp.broadcast_to(row, (NP, W))
    row = jnp.concatenate([b_ref[0:1, :], b_ref[1:2, :]], axis=1)
    out_ref[pl.ds(4, NP, stride=M1), :] = jnp.broadcast_to(row, (NP, W))
    block.wait()


def second_kernel(t_ref, a_ref, r1_ref, out_ref, cc_ref, c_ref, sec_ref, gram_ref):
    ia, ja = coords()
    p = ia * NJ + ja
    for q in range(4):
        rows = r1_ref[pl.ds(q, NP, stride=M1), :]
        other = turned(rows)
        c_ref[pl.ds(q, NP, stride=8), :] = join(rows, other)
        c_ref[pl.ds(q + 4, NP, stride=8), :] = join(other, rows)
    c = c_ref[...]
    a = a_ref[...]
    aa = jnp.concatenate([a, a], axis=1)
    cc = parts(c)
    cc_ref[...] = cc
    gram_a = dot_exact(a, aa, ((0,), (0,)))
    gram_c = dot(cc, cc, ((0,), (0,)))
    gram_ref[...] = gram_a * twice(gram_c[:R, :] + gram_c[R:, :])
    sec_ref[...] = aa
    weights = [parts(c * sec_ref[pl.ds(NI * ia + i, 1), :]) for i in range(NI)]
    second = None
    for i in range(NI):
        t_hi, t_lo = split(t_ref[i])
        part = dot(t_hi, weights[i]) + dot(t_lo, weights[i])
        second = part if second is None else second + part
    row = join(gram_ref[pl.ds(2 * p, 1), :], gram_ref[pl.ds(2 * p + 1, 1), :])
    out_ref[pl.ds(8, NK, stride=M2), :] = jnp.broadcast_to(row, (NK, W))
    for i in range(NI):
        row = r1_ref[pl.ds((i * NJ + ja) * M1 + 4, 1), :]
        out_ref[pl.ds(i, NK, stride=M2), :] = jnp.broadcast_to(row, (NK, W))
    c_ref[...] = second
    for i in range(NI):
        even = c_ref[pl.ds(i * 2 * NK, NK, stride=2), :]
        odd = c_ref[pl.ds(i * 2 * NK + 1, NK, stride=2), :]
        out_ref[pl.ds(4 + i, NK, stride=M2), :] = join(twice(even), twice(odd))


def third_kernel(t_ref, a_ref, cc_ref, r1_ref, r2_ref, out_ref, b_ref, third_ref):
    ia, ja = coords()
    p = ia * NJ + ja
    for i in range(NI):
        rows = r2_ref[pl.ds(i, NK, stride=M2), :]
        other = turned(rows)
        b_ref[pl.ds(i * 2 * NK, NK, stride=2), :] = join(rows, other)
        b_ref[pl.ds(i * 2 * NK + 1, NK, stride=2), :] = join(other, rows)
    b = b_ref[...]
    a = a_ref[pl.ds(NI * ia, NI), :]
    aa = jnp.concatenate([a, a], axis=1)
    a_turned = jnp.concatenate([aa, aa], axis=0).T[:R, :]
    bt = b.T[:R, :]
    third = None
    for i in range(NI):
        x = jnp.concatenate(split(bt * a_turned[:, i : i + 1]), axis=0)
        t_hi, t_lo = split(t_ref[i])
        part = dot(x, t_hi) + dot(x, t_lo)
        third = part if third is None else third + part
    gram_b = dot(jnp.concatenate(split(bt), axis=0), parts(b))
    gram_b = twice(gram_b[:R, :] + gram_b[R:, :])
    gram_a = a_turned[:, 0:1] * aa[0:1, :]
    for i in range(1, NI):
        gram_a = gram_a + a_turned[:, i : i + 1] * aa[i : i + 1, :]
    gram = parts(gram_a * gram_b)
    row = jnp.sum(r2_ref[pl.ds(8, NK, stride=M2), :], axis=0, keepdims=True)
    place = lax.broadcasted_iota(jnp.int32, (R, R), 0)
    mine = jnp.where(place == 2 * p, row[:, :R], jnp.where(place == 2 * p + 1, row[:, R:], 0.0))
    rows = r1_ref[pl.ds(4, NP, stride=M1), :]
    grad_b = dot_exact(jnp.concatenate([rows[:, :R], rows[:, R:]], axis=0), mine, ((1,), (0,)))
    grad_b = jnp.concatenate([grad_b[:NP, :], grad_b[NP:, :]], axis=1)
    summed = jnp.concatenate(
        [
            jnp.broadcast_to(
                jnp.sum(r2_ref[pl.ds(4 + i, NK, stride=M2), :], axis=0, keepdims=True), (NJ, W)
            )
            for i in range(NI)
        ],
        axis=0,
    )
    peer = lax.broadcasted_iota(jnp.int32, (NP, W), 0)
    grad_b = grad_b - jnp.where(lax.rem(peer, NJ) == ja, summed, 0.0)
    out_ref[pl.ds(4, NP, stride=M3), :] = grad_b
    third_ref[...] = twice(dot(cc_ref[...], jnp.concatenate([gram, gram], axis=0)) - third.T)
    for q in range(4):
        left = third_ref[pl.ds(q, NP, stride=8), :]
        right = third_ref[pl.ds(q + 4, NP, stride=8), :]
        out_ref[pl.ds(q, NP, stride=M3), :] = join(left, right)


def final_kernel(r3_ref, gb_ref, gc_ref):
    for q in range(4):
        row = jnp.sum(r3_ref[pl.ds(q, NP, stride=M3), :], axis=0, keepdims=True)
        gc_ref[q : q + 1, :] = row[:, :R]
        gc_ref[q + 4 : q + 5, :] = row[:, R:]
    row = jnp.sum(r3_ref[pl.ds(4, NP, stride=M3), :], axis=0, keepdims=True)
    gb_ref[0:1, :] = row[:, :R]
    gb_ref[1:2, :] = row[:, R:]


def call(kernel, outs, operands, scratch=(), copies=0, in_hbm=0, kinds=None):
    kinds = kinds or [F32] * len(outs)
    scratch_shapes = [pltpu.VMEM(shape, F32) for shape in scratch]
    if copies:
        scratch_shapes.append(pltpu.SemaphoreType.DMA((copies,)))
    return pl.pallas_call(
        kernel,
        out_shape=[jax.ShapeDtypeStruct(shape, kind) for shape, kind in zip(outs, kinds)],
        in_specs=[HBM] * in_hbm + [VMEM] * (len(operands) - in_hbm),
        out_specs=[VMEM] * len(outs),
        scratch_shapes=scratch_shapes,
        compiler_params=pltpu.CompilerParams(vmem_limit_bytes=16 * 1024 * 1024),
    )(*[pltpu.with_memory_space_constraint(x, pltpu.HBM) for x in operands[:in_hbm]], *operands[in_hbm:])


def exchange(x, axes, rows):
    peers = x.shape[0] // rows
    x = x.reshape(peers, rows, 1, W)
    x = lax.all_to_all(x, axes, 0, 0)
    return x.reshape(peers * rows, W)


def per_device(tensor, factor_a, factor_b, factor_c):
    s1, block = call(
        pack_kernel,
        [(NP * M1, W), tensor.shape],
        (factor_b, factor_c, tensor),
        [(2, R), (8, R)],
        copies=3,
        in_hbm=3,
    )
    r1 = exchange(s1, ("ia", "ja"), M1)
    s2, cc = call(
        second_kernel,
        [(NK * M2, W), (ROWS, W)],
        (block, factor_a, r1),
        [(ROWS, W), (16, W), (R, W)],
        kinds=[F32, BF16],
    )
    r2 = exchange(s2, "ka", M2)
    (s3,) = call(
        third_kernel,
        [(NP * M3, W)],
        (block, factor_a, cc, r1, r2),
        [(ROWS, W), (ROWS, W)],
    )
    r3 = exchange(s3, ("ia", "ja"), M3)
    return tuple(call(final_kernel, [(2, R), (8, R)], (r3,)))


def solution(mesh):
    placed = (P("ia", "ja", "ka"), P(), P(("ja", "ia", "ka"), None), P(("ka", "ia", "ja"), None))
    return jax.shard_map(
        per_device,
        mesh=mesh,
        in_specs=placed,
        out_specs=(P(("ja", "ia", "ka"), None), P(("ka", "ia", "ja"), None)),
        check_vma=False,
    )
```

time: 68.1 us -> 67.7 us (level)
  no operation moved by 1% of the time
where the time goes in v3:
time: 67.7 us; the launch traced here: 67.5 us
  blocking collectives  63.4 us (94%)
  Pallas kernels  3.43 us (5%)
    all_to_all x3, blocking collectives, exchange(): x = lax.all_to_all(x, axes, 0, 0)  63.4 us
    pallas_call x4, Pallas kernels, call(): pl.pallas_call(kernel, out_shape=[jax.ShapeDtypeStruct(shape, kind) for s...  3.43 us

profile of v3, /device:TPU:1, one launch (start us, length us, event | category | flops | bytes accessed | tf_op | source)
XLA Modules:
  0.0 67.5 jit_solution(3014969462668143078)
XLA Ops:
  0.6 1.3 %shard_map.59 = (f32[160,128]{1,0:T(8,128)S(1)}, f32[4,256,256]{2,1,0:T(8,128)S(1)}) custom-call(f32[2,64]{1,0:T(2,128)} %b_hbm.1, f32[8,64]{1,0:T(8,128)} %c_hbm.1, f32[4,256,256]{2,1,0:T(8,128)} %t_hbm.1), custom_call_target="tpu_custom_call" | custom-call | tf_op jit(solution)/shard_map/pallas_call | solution.py:183
  1.9 0.0 copy-start
  1.9 25.2 %all_to_all.15 = f32[32,5,1,128]{3,2,1,0:T(1,128)S(1)} all-to-all(f32[32,5,1,128]{3,2,1,0:T(1,128)S(1)} %bitcast.12), channel_id=1, replica_groups=mesh['ia'=4,'ja'=8,'ka'=32] {'ia','ja'}, dimensions={0} | all-to-all | bytes 163840 | tf_op jit(solution)/shard_map/all_to_all | solution.py:196
  27.1 0.0 copy-done
  27.1 0.7 %shard_map.60 = (f32[288,128]{1,0:T(8,128)S(1)}, bf16[256,128]{1,0:T(8,128)(2,1)S(1)}) custom-call(f32[4,256,256]{2,1,0:T(8,128)S(1)} %get-tuple-element.6.t_ref, f32[16,64]{1,0:T(8,128)S(1)} %copy-done, f32[160,128]{1,0:T(8,128)S(1)} %bitcast.6), custom_call_target="tpu_custom_call" | custom-call | tf_op jit(solution)/shard_map/pallas_call | solution.py:183
  27.8 25.0 %all_to_all.16 = f32[32,9,1,128]{3,2,1,0:T(1,128)S(1)} all-to-all(f32[32,9,1,128]{3,2,1,0:T(1,128)S(1)} %bitcast.11), channel_id=1, replica_groups=mesh['ia'=4,'ja'=8,'ka'=32] {'ka'}, dimensions={0} | all-to-all | bytes 294912 | tf_op jit(solution)/shard_map/all_to_all | solution.py:196
  52.7 0.8 %shard_map.61 = f32[160,128]{1,0:T(8,128)S(1)} custom-call(f32[4,256,256]{2,1,0:T(8,128)S(1)} %get-tuple-element.6.t_ref, f32[16,64]{1,0:T(8,128)S(1)} %copy-done, bf16[256,128]{1,0:T(8,128)(2,1)S(1)} %get-tuple-element.8.cc_ref, f32[160,128]{1,0:T(8,128)S(1)} %bitcast.7, f32[288,128]{1,0:T(8,128)S(1)} %bitcast.8), custom_call_target="tpu_custom_call" | custom-call | tf_op jit(solution)/shard_map/pallas_call | solution.py:183
  53.5 13.2 %all_to_all.17 = f32[32,5,1,128]{3,2,1,0:T(1,128)S(1)} all-to-all(f32[32,5,1,128]{3,2,1,0:T(1,128)S(1)} %bitcast.9), channel_id=1, replica_groups=mesh['ia'=4,'ja'=8,'ka'=32] {'ia','ja'}, dimensions={0} | all-to-all | bytes 163840 | tf_op jit(solution)/shard_map/all_to_all | solution.py:196
  66.8 0.7 shard_map.62
Async XLA Ops:
  1.9 25.2 %copy-start = (f32[16,64]{1,0:T(8,128)S(1)}, f32[16,64]{1,0:T(8,128)}, u32[]{:S(2)}) copy-start(f32[16,64]{1,0:T(8,128)} %a_ref.3) | copy-start | bytes 12292

commit v4 on v3

--- a/solution.py
+++ b/solution.py
@@ -67,8 +67,7 @@
     return copy
 
 
-def pack_kernel(b_hbm, c_hbm, t_hbm, out_ref, t_ref, b_ref, c_ref, sems):
-    block = fetch(t_hbm, t_ref, sems.at[2])
+def pack_kernel(b_hbm, c_hbm, out_ref, b_ref, c_ref, sems):
     copies = [fetch(b_hbm, b_ref, sems.at[0]), fetch(c_hbm, c_ref, sems.at[1])]
     for copy in copies:
         copy.wait()
@@ -77,7 +76,6 @@
         out_ref[pl.ds(q, NP, stride=M1), :] = jnp.broadcast_to(row, (NP, W))
     row = jnp.concatenate([b_ref[0:1, :], b_ref[1:2, :]], axis=1)
     out_ref[pl.ds(4, NP, stride=M1), :] = jnp.broadcast_to(row, (NP, W))
-    block.wait()
 
 
 def second_kernel(t_ref, a_ref, r1_ref, out_ref, cc_ref, c_ref, sec_ref, gram_ref):
@@ -187,6 +185,7 @@
         out_specs=[VMEM] * len(outs),
         scratch_shapes=scratch_shapes,
         compiler_params=pltpu.CompilerParams(vmem_limit_bytes=16 * 1024 * 1024),
+        cost_estimate=pl.CostEstimate(flops=10**9, bytes_accessed=NP * M1 * W * 4, transcendentals=0),
     )(*[pltpu.with_memory_space_constraint(x, pltpu.HBM) for x in operands[:in_hbm]], *operands[in_hbm:])
 
 
@@ -198,14 +197,20 @@
 
 
 def per_device(tensor, factor_a, factor_b, factor_c):
-    s1, block = call(
+    s1 = pl.pallas_call(
         pack_kernel,
-        [(NP * M1, W), tensor.shape],
-        (factor_b, factor_c, tensor),
-        [(2, R), (8, R)],
-        copies=3,
-        in_hbm=3,
-    )
+        out_shape=pltpu.VMEM((NP * M1, W), F32),
+        in_specs=[HBM] * 2,
+        out_specs=VMEM,
+        scratch_shapes=[
+            pltpu.VMEM((2, R), F32),
+            pltpu.VMEM((8, R), F32),
+            pltpu.SemaphoreType.DMA((2,)),
+        ],
+        compiler_params=pltpu.CompilerParams(vmem_limit_bytes=16 * 1024 * 1024),
+        cost_estimate=pl.CostEstimate(flops=10**9, bytes_accessed=NP * M1 * W * 4, transcendentals=0),
+    )(*[pltpu.with_memory_space_constraint(x, pltpu.HBM) for x in (factor_b, factor_c)])
+    block = tensor
     r1 = exchange(s1, ("ia", "ja"), M1)
     s2, cc = call(
         second_kernel,

time: 67.7 us -> 67.6 us (level)
    pallas_call x4 -> x3, Pallas kernels: 3.43 us -> 2.18 us  [call(): pl.pallas_call(kernel, out_shape=[jax.ShapeDtypeStruct(shape, kind) for s...]
    pallas_call x0 -> x1, Pallas kernels: none -> 0.88 us  [per_device(): pl.pallas_call(pack_kernel, out_shape=pltpu.VMEM((NP * M1, W), F32), in_s...]
where the time goes in v4:
time: 67.6 us; the launch traced here: 67.3 us
  blocking collectives  63.6 us (94%)
  Pallas kernels  3.06 us (5%)
    all_to_all x3, blocking collectives, exchange(): x = lax.all_to_all(x, axes, 0, 0)  63.6 us
    pallas_call x3, Pallas kernels, call(): pl.pallas_call(kernel, out_shape=[jax.ShapeDtypeStruct(shape, kind) for s...  2.18 us

profile of v4, /device:TPU:1, one launch (start us, length us, event | category | flops | bytes accessed | tf_op | source)
XLA Modules:
  0.0 67.3 jit_solution(3055082219998462049)
XLA Ops:
  0.6 0.0 copy-start
  0.6 0.9 %shard_map.59 = f32[160,128]{1,0:T(8,128)S(1)} custom-call(f32[2,64]{1,0:T(2,128)} %b_hbm.1, f32[8,64]{1,0:T(8,128)} %c_hbm.1), custom_call_target="tpu_custom_call" | custom-call | flops 1000000000 | bytes 81920 | tf_op jit(solution)/shard_map/pallas_call | solution.py:200
  1.5 0.0 copy-start.1
  1.5 25.2 %all_to_all.15 = f32[32,5,1,128]{3,2,1,0:T(1,128)S(1)} all-to-all(f32[32,5,1,128]{3,2,1,0:T(1,128)S(1)} %bitcast.12), channel_id=1, replica_groups=mesh['ia'=4,'ja'=8,'ka'=32] {'ia','ja'}, dimensions={0} | all-to-all | bytes 163840 | tf_op jit(solution)/shard_map/all_to_all | solution.py:195
  26.7 0.0 copy-done
  26.7 0.0 copy-done.1
  26.7 0.7 %shard_map.60 = (f32[288,128]{1,0:T(8,128)S(1)}, bf16[256,128]{1,0:T(8,128)(2,1)S(1)}) custom-call(f32[4,256,256]{2,1,0:T(8,128)S(1)} %copy-done, f32[16,64]{1,0:T(8,128)S(1)} %copy-done.1, f32[160,128]{1,0:T(8,128)S(1)} %bitcast.8), custom_call_target="tpu_custom_call" | custom-call | flops 1000000000 | bytes 81920 | tf_op jit(solution)/shard_map/pallas_call | solution.py:181
  27.4 25.2 %all_to_all.16 = f32[32,9,1,128]{3,2,1,0:T(1,128)S(1)} all-to-all(f32[32,9,1,128]{3,2,1,0:T(1,128)S(1)} %bitcast.7), channel_id=1, replica_groups=mesh['ia'=4,'ja'=8,'ka'=32] {'ka'}, dimensions={0} | all-to-all | bytes 294912 | tf_op jit(solution)/shard_map/all_to_all | solution.py:195
  52.6 0.8 %shard_map.61 = f32[160,128]{1,0:T(8,128)S(1)} custom-call(f32[4,256,256]{2,1,0:T(8,128)S(1)} %copy-done, f32[16,64]{1,0:T(8,128)S(1)} %copy-done.1, bf16[256,128]{1,0:T(8,128)(2,1)S(1)} %get-tuple-element.4.cc_ref, f32[160,128]{1,0:T(8,128)S(1)} %bitcast.9, f32[288,128]{1,0:T(8,128)S(1)} %bitcast.6), custom_call_target="tpu_custom_call" | custom-call | flops 1000000000 | bytes 81920 | tf_op jit(solution)/shard_map/pallas_call | solution.py:181
  53.4 13.2 %all_to_all.17 = f32[32,5,1,128]{3,2,1,0:T(1,128)S(1)} all-to-all(f32[32,5,1,128]{3,2,1,0:T(1,128)S(1)} %bitcast.10), channel_id=1, replica_groups=mesh['ia'=4,'ja'=8,'ka'=32] {'ia','ja'}, dimensions={0} | all-to-all | bytes 163840 | tf_op jit(solution)/shard_map/all_to_all | solution.py:195
  66.7 0.7 %shard_map.62 = (f32[2,64]{1,0:T(2,128)}, f32[8,64]{1,0:T(8,128)}) custom-call(f32[160,128]{1,0:T(8,128)S(1)} %bitcast.11), custom_call_target="tpu_custom_call" | custom-call | flops 1000000000 | bytes 81920 | tf_op jit(solution)/shard_map/pallas_call | solution.py:181
Async XLA Ops:
  0.6 26.1 %copy-start = (f32[4,256,256]{2,1,0:T(8,128)S(1)}, f32[4,256,256]{2,1,0:T(8,128)}, u32[]{:S(2)}) copy-start(f32[4,256,256]{2,1,0:T(8,128)} %t_ref.3) | copy-start | bytes 3145732
  1.5 25.2 %copy-start.1 = (f32[16,64]{1,0:T(8,128)S(1)}, f32[16,64]{1,0:T(8,128)}, u32[]{:S(2)}) copy-start(f32[16,64]{1,0:T(8,128)} %a_ref.3) | copy-start | bytes 12292

commit v5 on v4

--- a/solution.py
+++ b/solution.py
@@ -16,6 +16,7 @@
 W = 2 * R
 ROWS = 256
 M1, M2, M3 = 5, 9, 5
+HEAD_P, HEAD_K = 4, 30
 
 
 def coords():
@@ -42,6 +43,15 @@
 
 def join(x, y):
     return jnp.where(left_half(x), x, y)
+
+
+def slot(p):
+    return jnp.where(p == 0, HEAD_P, jnp.where(p == HEAD_P, 0, p))
+
+
+def swapped(x):
+    head = 8 * HEAD_P
+    return jnp.concatenate([x[head : head + 8], x[8:head], x[:8], x[head + 8 :]], axis=0)
 
 
 def turned(x):
@@ -86,7 +96,7 @@
         other = turned(rows)
         c_ref[pl.ds(q, NP, stride=8), :] = join(rows, other)
         c_ref[pl.ds(q + 4, NP, stride=8), :] = join(other, rows)
-    c = c_ref[...]
+    c = swapped(c_ref[...])
     a = a_ref[...]
     aa = jnp.concatenate([a, a], axis=1)
     cc = parts(c)
@@ -104,13 +114,17 @@
     row = join(gram_ref[pl.ds(2 * p, 1), :], gram_ref[pl.ds(2 * p + 1, 1), :])
     out_ref[pl.ds(8, NK, stride=M2), :] = jnp.broadcast_to(row, (NK, W))
     for i in range(NI):
-        row = r1_ref[pl.ds((i * NJ + ja) * M1 + 4, 1), :]
+        row = r1_ref[pl.ds(slot(i * NJ + ja) * M1 + 4, 1), :]
         out_ref[pl.ds(i, NK, stride=M2), :] = jnp.broadcast_to(row, (NK, W))
     c_ref[...] = second
     for i in range(NI):
         even = c_ref[pl.ds(i * 2 * NK, NK, stride=2), :]
         odd = c_ref[pl.ds(i * 2 * NK + 1, NK, stride=2), :]
         out_ref[pl.ds(4 + i, NK, stride=M2), :] = join(twice(even), twice(odd))
+    head = HEAD_K * M2
+    first, last = out_ref[4:8, :], out_ref[head + 4 : head + 8, :]
+    out_ref[4:8, :] = last
+    out_ref[head + 4 : head + 8, :] = first
 
 
 def third_kernel(t_ref, a_ref, cc_ref, r1_ref, r2_ref, out_ref, b_ref, third_ref):
@@ -121,6 +135,11 @@
         other = turned(rows)
         b_ref[pl.ds(i * 2 * NK, NK, stride=2), :] = join(rows, other)
         b_ref[pl.ds(i * 2 * NK + 1, NK, stride=2), :] = join(other, rows)
+        for ka, place in ((0, HEAD_K), (HEAD_K, 0)):
+            row = r2_ref[place * M2 + i : place * M2 + i + 1, :]
+            start = i * 2 * NK + 2 * ka
+            b_ref[start : start + 1, :] = join(row, turned(row))
+            b_ref[start + 1 : start + 2, :] = join(turned(row), row)
     b = b_ref[...]
     a = a_ref[pl.ds(NI * ia, NI), :]
     aa = jnp.concatenate([a, a], axis=1)
@@ -153,10 +172,11 @@
         ],
         axis=0,
     )
-    peer = lax.broadcasted_iota(jnp.int32, (NP, W), 0)
+    peer = slot(lax.broadcasted_iota(jnp.int32, (NP, W), 0))
     grad_b = grad_b - jnp.where(lax.rem(peer, NJ) == ja, summed, 0.0)
     out_ref[pl.ds(4, NP, stride=M3), :] = grad_b
-    third_ref[...] = twice(dot(cc_ref[...], jnp.concatenate([gram, gram], axis=0)) - third.T)
+    third = twice(dot(cc_ref[...], jnp.concatenate([gram, gram], axis=0)) - third.T)
+    third_ref[...] = swapped(third)
     for q in range(4):
         left = third_ref[pl.ds(q, NP, stride=8), :]
         right = third_ref[pl.ds(q + 4, NP, stride=8), :]
@@ -189,10 +209,12 @@
     )(*[pltpu.with_memory_space_constraint(x, pltpu.HBM) for x in operands[:in_hbm]], *operands[in_hbm:])
 
 
-def exchange(x, axes, rows):
+def exchange(x, axes, rows, head):
     peers = x.shape[0] // rows
+    order = list(range(peers))
+    order[0], order[head] = head, 0
     x = x.reshape(peers, rows, 1, W)
-    x = lax.all_to_all(x, axes, 0, 0)
+    x = lax.all_to_all(x, axes, 0, 0, axis_index_groups=[order])
     return x.reshape(peers * rows, W)
 
 
@@ -211,7 +233,7 @@
         cost_estimate=pl.CostEstimate(flops=10**9, bytes_accessed=NP * M1 * W * 4, transcendentals=0),
     )(*[pltpu.with_memory_space_constraint(x, pltpu.HBM) for x in (factor_b, factor_c)])
     block = tensor
-    r1 = exchange(s1, ("ia", "ja"), M1)
+    r1 = exchange(s1, ("ia", "ja"), M1, HEAD_P)
     s2, cc = call(
         second_kernel,
         [(NK * M2, W), (ROWS, W)],
@@ -219,14 +241,14 @@
         [(ROWS, W), (16, W), (R, W)],
         kinds=[F32, BF16],
     )
-    r2 = exchange(s2, "ka", M2)
+    r2 = exchange(s2, "ka", M2, HEAD_K)
     (s3,) = call(
         third_kernel,
         [(NP * M3, W)],
         (block, factor_a, cc, r1, r2),
         [(ROWS, W), (ROWS, W)],
     )
-    r3 = exchange(s3, ("ia", "ja"), M3)
+    r3 = exchange(s3, ("ia", "ja"), M3, HEAD_P)
     return tuple(call(final_kernel, [(2, R), (8, R)], (r3,)))
 
 

time: 67.6 us -> 59.1 us (0.87)
  blocking collectives: 63.6 us -> 55.1 us
    all_to_all x3, blocking collectives: 63.6 us -> 55.1 us  [exchange(): x = lax.all_to_all(x, axes, 0, 0, axis_index_groups=[order])]
where the time goes in v5:
time: 59.1 us; the launch traced here: 58.9 us
  blocking collectives  55.1 us (93%)
  Pallas kernels  3.07 us (5%)
  between operations  0.66 us (1%)
    all_to_all x3, blocking collectives, exchange(): x = lax.all_to_all(x, axes, 0, 0, axis_index_groups=[order])  55.1 us
    pallas_call x3, Pallas kernels, call(): pl.pallas_call(kernel, out_shape=[jax.ShapeDtypeStruct(shape, kind) for s...  2.18 us

profile of v5, /device:TPU:1, one launch (start us, length us, event | category | flops | bytes accessed | tf_op | source)
XLA Modules:
  0.0 58.9 jit_solution(6474805215724443126)
XLA Ops:
  0.6 0.0 copy-start
  0.6 0.9 %shard_map.59 = f32[160,128]{1,0:T(8,128)S(1)} custom-call(f32[2,64]{1,0:T(2,128)} %b_hbm.1, f32[8,64]{1,0:T(8,128)} %c_hbm.1), custom_call_target="tpu_custom_call" | custom-call | flops 1000000000 | bytes 81920 | tf_op jit(solution)/shard_map/pallas_call | solution.py:222
  1.5 0.0 copy-start.1
  1.5 24.4 %all_to_all.15 = f32[32,5,1,128]{3,2,1,0:T(1,128)S(1)} all-to-all(f32[32,5,1,128]{3,2,1,0:T(1,128)S(1)} %bitcast.12), channel_id=1, replica_groups={{128,32,64,96,0,160,192,224,256,288,320,352,384,416,448,480,512,544,576..., dimensions={0} | all-to-all | bytes 163840 | tf_op jit(solution)/shard_map/all_to_all | solution.py:217
  26.0 0.0 copy-done
  26.0 0.0 copy-done.1
  26.0 0.7 %shard_map.60 = (f32[288,128]{1,0:T(8,128)S(1)}, bf16[256,128]{1,0:T(8,128)(2,1)S(1)}) custom-call(f32[4,256,256]{2,1,0:T(8,128)S(1)} %copy-done, f32[16,64]{1,0:T(8,128)S(1)} %copy-done.1, f32[160,128]{1,0:T(8,128)S(1)} %bitcast.8), custom_call_target="tpu_custom_call" | custom-call | flops 1000000000 | bytes 81920 | tf_op jit(solution)/shard_map/pallas_call | solution.py:201
  26.7 17.8 %all_to_all.16 = f32[32,9,1,128]{3,2,1,0:T(1,128)S(1)} all-to-all(f32[32,9,1,128]{3,2,1,0:T(1,128)S(1)} %bitcast.7), channel_id=1, replica_groups={{30,1,2,3,4,5,6,7,8,9,10,11,12,13,14,15,16,17,18,19,20,21,22,23,24,25,2..., dimensions={0} | all-to-all | bytes 294912 | tf_op jit(solution)/shard_map/all_to_all | solution.py:217
  44.5 0.8 %shard_map.61 = f32[160,128]{1,0:T(8,128)S(1)} custom-call(f32[4,256,256]{2,1,0:T(8,128)S(1)} %copy-done, f32[16,64]{1,0:T(8,128)S(1)} %copy-done.1, bf16[256,128]{1,0:T(8,128)(2,1)S(1)} %get-tuple-element.4.cc_ref, f32[160,128]{1,0:T(8,128)S(1)} %bitcast.9, f32[288,128]{1,0:T(8,128)S(1)} %bitcast.6), custom_call_target="tpu_custom_call" | custom-call | flops 1000000000 | bytes 81920 | tf_op jit(solution)/shard_map/pallas_call | solution.py:201
  45.3 12.8 %all_to_all.17 = f32[32,5,1,128]{3,2,1,0:T(1,128)S(1)} all-to-all(f32[32,5,1,128]{3,2,1,0:T(1,128)S(1)} %bitcast.10), channel_id=1, replica_groups={{128,32,64,96,0,160,192,224,256,288,320,352,384,416,448,480,512,544,576..., dimensions={0} | all-to-all | bytes 163840 | tf_op jit(solution)/shard_map/all_to_all | solution.py:217
  58.2 0.7 %shard_map.62 = (f32[2,64]{1,0:T(2,128)}, f32[8,64]{1,0:T(8,128)}) custom-call(f32[160,128]{1,0:T(8,128)S(1)} %bitcast.11), custom_call_target="tpu_custom_call" | custom-call | flops 1000000000 | bytes 81920 | tf_op jit(solution)/shard_map/pallas_call | solution.py:201
Async XLA Ops:
  0.6 25.4 %copy-start = (f32[4,256,256]{2,1,0:T(8,128)S(1)}, f32[4,256,256]{2,1,0:T(8,128)}, u32[]{:S(2)}) copy-start(f32[4,256,256]{2,1,0:T(8,128)} %t_ref.3) | copy-start | bytes 3145732
  1.5 24.5 %copy-start.1 = (f32[16,64]{1,0:T(8,128)S(1)}, f32[16,64]{1,0:T(8,128)}, u32[]{:S(2)}) copy-start(f32[16,64]{1,0:T(8,128)} %a_ref.3) | copy-start | bytes 12292

commit v6 on v5

--- a/solution.py
+++ b/solution.py
@@ -16,7 +16,7 @@
 W = 2 * R
 ROWS = 256
 M1, M2, M3 = 5, 9, 5
-HEAD_P, HEAD_K = 4, 30
+HEAD_P, HEAD_K = 12, 26
 
 
 def coords():
@@ -163,17 +163,10 @@
     rows = r1_ref[pl.ds(4, NP, stride=M1), :]
     grad_b = dot_exact(jnp.concatenate([rows[:, :R], rows[:, R:]], axis=0), mine, ((1,), (0,)))
     grad_b = jnp.concatenate([grad_b[:NP, :], grad_b[NP:, :]], axis=1)
-    summed = jnp.concatenate(
-        [
-            jnp.broadcast_to(
-                jnp.sum(r2_ref[pl.ds(4 + i, NK, stride=M2), :], axis=0, keepdims=True), (NJ, W)
-            )
-            for i in range(NI)
-        ],
-        axis=0,
-    )
     peer = slot(lax.broadcasted_iota(jnp.int32, (NP, W), 0))
-    grad_b = grad_b - jnp.where(lax.rem(peer, NJ) == ja, summed, 0.0)
+    for i in range(NI):
+        row = jnp.sum(r2_ref[pl.ds(4 + i, NK, stride=M2), :], axis=0, keepdims=True)
+        grad_b = grad_b - jnp.where(peer == i * NJ + ja, row, 0.0)
     out_ref[pl.ds(4, NP, stride=M3), :] = grad_b
     third = twice(dot(cc_ref[...], jnp.concatenate([gram, gram], axis=0)) - third.T)
     third_ref[...] = swapped(third)

time: 59.1 us -> 58.2 us (0.985)
  blocking collectives: 55.1 us -> 54.2 us
    all_to_all x3, blocking collectives: 55.1 us -> 54.2 us  [exchange(): x = lax.all_to_all(x, axes, 0, 0, axis_index_groups=[order])]
where the time goes in v6:
time: 58.2 us; the launch traced here: 57.9 us
  blocking collectives  54.2 us (93%)
  Pallas kernels  3.05 us (5%)
  between operations  0.66 us (1%)
    all_to_all x3, blocking collectives, exchange(): x = lax.all_to_all(x, axes, 0, 0, axis_index_groups=[order])  54.2 us
    pallas_call x3, Pallas kernels, call(): pl.pallas_call(kernel, out_shape=[jax.ShapeDtypeStruct(shape, kind) for s...  2.17 us

profile of v6, /device:TPU:1, one launch (start us, length us, event | category | flops | bytes accessed | tf_op | source)
XLA Modules:
  0.0 57.9 jit_solution(5662482848930536655)
XLA Ops:
  0.6 0.0 copy-start
  0.6 0.9 %shard_map.59 = f32[160,128]{1,0:T(8,128)S(1)} custom-call(f32[2,64]{1,0:T(2,128)} %b_hbm.1, f32[8,64]{1,0:T(8,128)} %c_hbm.1), custom_call_target="tpu_custom_call" | custom-call | flops 1000000000 | bytes 81920 | tf_op jit(solution)/shard_map/pallas_call | solution.py:215
  1.5 0.0 copy-start.1
  1.5 24.1 %all_to_all.15 = f32[32,5,1,128]{3,2,1,0:T(1,128)S(1)} all-to-all(f32[32,5,1,128]{3,2,1,0:T(1,128)S(1)} %bitcast.12), channel_id=1, replica_groups={{384,32,64,96,128,160,192,224,256,288,320,352,0,416,448,480,512,544,576..., dimensions={0} | all-to-all | bytes 163840 | tf_op jit(solution)/shard_map/all_to_all | solution.py:210
  25.6 0.0 copy-done
  25.6 0.0 copy-done.1
  25.6 0.7 %shard_map.60 = (f32[288,128]{1,0:T(8,128)S(1)}, bf16[256,128]{1,0:T(8,128)(2,1)S(1)}) custom-call(f32[4,256,256]{2,1,0:T(8,128)S(1)} %copy-done, f32[16,64]{1,0:T(8,128)S(1)} %copy-done.1, f32[160,128]{1,0:T(8,128)S(1)} %bitcast.8), custom_call_target="tpu_custom_call" | custom-call | flops 1000000000 | bytes 81920 | tf_op jit(solution)/shard_map/pallas_call | solution.py:194
  26.3 17.6 %all_to_all.16 = f32[32,9,1,128]{3,2,1,0:T(1,128)S(1)} all-to-all(f32[32,9,1,128]{3,2,1,0:T(1,128)S(1)} %bitcast.7), channel_id=1, replica_groups={{26,1,2,3,4,5,6,7,8,9,10,11,12,13,14,15,16,17,18,19,20,21,22,23,24,25,0..., dimensions={0} | all-to-all | bytes 294912 | tf_op jit(solution)/shard_map/all_to_all | solution.py:210
  43.9 0.8 %shard_map.61 = f32[160,128]{1,0:T(8,128)S(1)} custom-call(f32[4,256,256]{2,1,0:T(8,128)S(1)} %copy-done, f32[16,64]{1,0:T(8,128)S(1)} %copy-done.1, bf16[256,128]{1,0:T(8,128)(2,1)S(1)} %get-tuple-element.4.cc_ref, f32[160,128]{1,0:T(8,128)S(1)} %bitcast.9, f32[288,128]{1,0:T(8,128)S(1)} %bitcast.6), custom_call_target="tpu_custom_call" | custom-call | flops 1000000000 | bytes 81920 | tf_op jit(solution)/shard_map/pallas_call | solution.py:194
  44.7 12.5 %all_to_all.17 = f32[32,5,1,128]{3,2,1,0:T(1,128)S(1)} all-to-all(f32[32,5,1,128]{3,2,1,0:T(1,128)S(1)} %bitcast.10), channel_id=1, replica_groups={{384,32,64,96,128,160,192,224,256,288,320,352,0,416,448,480,512,544,576..., dimensions={0} | all-to-all | bytes 163840 | tf_op jit(solution)/shard_map/all_to_all | solution.py:210
  57.2 0.7 %shard_map.62 = (f32[2,64]{1,0:T(2,128)}, f32[8,64]{1,0:T(8,128)}) custom-call(f32[160,128]{1,0:T(8,128)S(1)} %bitcast.11), custom_call_target="tpu_custom_call" | custom-call | flops 1000000000 | bytes 81920 | tf_op jit(solution)/shard_map/pallas_call | solution.py:194
Async XLA Ops:
  0.6 25.0 %copy-start = (f32[4,256,256]{2,1,0:T(8,128)S(1)}, f32[4,256,256]{2,1,0:T(8,128)}, u32[]{:S(2)}) copy-start(f32[4,256,256]{2,1,0:T(8,128)} %t_ref.3) | copy-start | bytes 3145732
  1.5 24.1 %copy-start.1 = (f32[16,64]{1,0:T(8,128)S(1)}, f32[16,64]{1,0:T(8,128)}, u32[]{:S(2)}) copy-start(f32[16,64]{1,0:T(8,128)} %a_ref.3) | copy-start | bytes 12292

commit v7 on v6

--- a/solution.py
+++ b/solution.py
@@ -16,7 +16,7 @@
 W = 2 * R
 ROWS = 256
 M1, M2, M3 = 5, 9, 5
-HEAD_P, HEAD_K = 12, 26
+HEAD_P, HEAD_K = 13, 26
 
 
 def coords():

time: 58.2 us -> 58.4 us (level)
  no operation moved by 1% of the time
where the time goes in v7:
time: 58.4 us; the launch traced here: 58.1 us
  blocking collectives  54.4 us (93%)
  Pallas kernels  3.05 us (5%)
  between operations  0.66 us (1%)
    all_to_all x3, blocking collectives, exchange(): x = lax.all_to_all(x, axes, 0, 0, axis_index_groups=[order])  54.4 us
    pallas_call x3, Pallas kernels, call(): pl.pallas_call(kernel, out_shape=[jax.ShapeDtypeStruct(shape, kind) for s...  2.17 us

profile of v7, /device:TPU:1, one launch (start us, length us, event | category | flops | bytes accessed | tf_op | source)
XLA Modules:
  0.0 58.1 jit_solution(855911303756115157)
XLA Ops:
  0.6 0.0 copy-start
  0.6 0.9 %shard_map.59 = f32[160,128]{1,0:T(8,128)S(1)} custom-call(f32[2,64]{1,0:T(2,128)} %b_hbm.1, f32[8,64]{1,0:T(8,128)} %c_hbm.1), custom_call_target="tpu_custom_call" | custom-call | flops 1000000000 | bytes 81920 | tf_op jit(solution)/shard_map/pallas_call | solution.py:215
  1.5 0.0 copy-start.1
  1.5 24.1 %all_to_all.15 = f32[32,5,1,128]{3,2,1,0:T(1,128)S(1)} all-to-all(f32[32,5,1,128]{3,2,1,0:T(1,128)S(1)} %bitcast.12), channel_id=1, replica_groups={{416,32,64,96,128,160,192,224,256,288,320,352,384,0,448,480,512,544,576..., dimensions={0} | all-to-all | bytes 163840 | tf_op jit(solution)/shard_map/all_to_all | solution.py:210
  25.7 0.0 copy-done
  25.7 0.0 copy-done.1
  25.7 0.7 %shard_map.60 = (f32[288,128]{1,0:T(8,128)S(1)}, bf16[256,128]{1,0:T(8,128)(2,1)S(1)}) custom-call(f32[4,256,256]{2,1,0:T(8,128)S(1)} %copy-done, f32[16,64]{1,0:T(8,128)S(1)} %copy-done.1, f32[160,128]{1,0:T(8,128)S(1)} %bitcast.8), custom_call_target="tpu_custom_call" | custom-call | flops 1000000000 | bytes 81920 | tf_op jit(solution)/shard_map/pallas_call | solution.py:194
  26.4 18.4 %all_to_all.16 = f32[32,9,1,128]{3,2,1,0:T(1,128)S(1)} all-to-all(f32[32,9,1,128]{3,2,1,0:T(1,128)S(1)} %bitcast.7), channel_id=1, replica_groups={{26,1,2,3,4,5,6,7,8,9,10,11,12,13,14,15,16,17,18,19,20,21,22,23,24,25,0..., dimensions={0} | all-to-all | bytes 294912 | tf_op jit(solution)/shard_map/all_to_all | solution.py:210
  44.8 0.8 %shard_map.61 = f32[160,128]{1,0:T(8,128)S(1)} custom-call(f32[4,256,256]{2,1,0:T(8,128)S(1)} %copy-done, f32[16,64]{1,0:T(8,128)S(1)} %copy-done.1, bf16[256,128]{1,0:T(8,128)(2,1)S(1)} %get-tuple-element.4.cc_ref, f32[160,128]{1,0:T(8,128)S(1)} %bitcast.9, f32[288,128]{1,0:T(8,128)S(1)} %bitcast.6), custom_call_target="tpu_custom_call" | custom-call | flops 1000000000 | bytes 81920 | tf_op jit(solution)/shard_map/pallas_call | solution.py:194
  45.6 11.9 %all_to_all.17 = f32[32,5,1,128]{3,2,1,0:T(1,128)S(1)} all-to-all(f32[32,5,1,128]{3,2,1,0:T(1,128)S(1)} %bitcast.10), channel_id=1, replica_groups={{416,32,64,96,128,160,192,224,256,288,320,352,384,0,448,480,512,544,576..., dimensions={0} | all-to-all | bytes 163840 | tf_op jit(solution)/shard_map/all_to_all | solution.py:210
  57.5 0.7 %shard_map.62 = (f32[2,64]{1,0:T(2,128)}, f32[8,64]{1,0:T(8,128)}) custom-call(f32[160,128]{1,0:T(8,128)S(1)} %bitcast.11), custom_call_target="tpu_custom_call" | custom-call | flops 1000000000 | bytes 81920 | tf_op jit(solution)/shard_map/pallas_call | solution.py:194
Async XLA Ops:
  0.6 25.1 %copy-start = (f32[4,256,256]{2,1,0:T(8,128)S(1)}, f32[4,256,256]{2,1,0:T(8,128)}, u32[]{:S(2)}) copy-start(f32[4,256,256]{2,1,0:T(8,128)} %t_ref.3) | copy-start | bytes 3145732
  1.5 24.2 %copy-start.1 = (f32[16,64]{1,0:T(8,128)S(1)}, f32[16,64]{1,0:T(8,128)}, u32[]{:S(2)}) copy-start(f32[16,64]{1,0:T(8,128)} %a_ref.3) | copy-start | bytes 12292

commit v8 on v7

--- a/solution.py
+++ b/solution.py
@@ -16,7 +16,7 @@
 W = 2 * R
 ROWS = 256
 M1, M2, M3 = 5, 9, 5
-HEAD_P, HEAD_K = 13, 26
+HEAD_P, HEAD_K = 12, 22
 
 
 def coords():

time: 58.4 us -> 58.2 us (level)
  no operation moved by 1% of the time
where the time goes in v8:
time: 58.2 us; the launch traced here: 57.9 us
  blocking collectives  54.2 us (93%)
  Pallas kernels  3.05 us (5%)
  between operations  0.66 us (1%)
    all_to_all x3, blocking collectives, exchange(): x = lax.all_to_all(x, axes, 0, 0, axis_index_groups=[order])  54.2 us
    pallas_call x3, Pallas kernels, call(): pl.pallas_call(kernel, out_shape=[jax.ShapeDtypeStruct(shape, kind) for s...  2.16 us

profile of v8, /device:TPU:1, one launch (start us, length us, event | category | flops | bytes accessed | tf_op | source)
XLA Modules:
  0.0 57.9 jit_solution(9493071437392309878)
XLA Ops:
  0.6 0.0 copy-start
  0.6 0.9 %shard_map.59 = f32[160,128]{1,0:T(8,128)S(1)} custom-call(f32[2,64]{1,0:T(2,128)} %b_hbm.1, f32[8,64]{1,0:T(8,128)} %c_hbm.1), custom_call_target="tpu_custom_call" | custom-call | flops 1000000000 | bytes 81920 | tf_op jit(solution)/shard_map/pallas_call | solution.py:215
  1.5 0.0 copy-start.1
  1.5 24.1 %all_to_all.15 = f32[32,5,1,128]{3,2,1,0:T(1,128)S(1)} all-to-all(f32[32,5,1,128]{3,2,1,0:T(1,128)S(1)} %bitcast.12), channel_id=1, replica_groups={{384,32,64,96,128,160,192,224,256,288,320,352,0,416,448,480,512,544,576..., dimensions={0} | all-to-all | bytes 163840 | tf_op jit(solution)/shard_map/all_to_all | solution.py:210
  25.6 0.0 copy-done
  25.6 0.0 copy-done.1
  25.6 0.7 %shard_map.60 = (f32[288,128]{1,0:T(8,128)S(1)}, bf16[256,128]{1,0:T(8,128)(2,1)S(1)}) custom-call(f32[4,256,256]{2,1,0:T(8,128)S(1)} %copy-done, f32[16,64]{1,0:T(8,128)S(1)} %copy-done.1, f32[160,128]{1,0:T(8,128)S(1)} %bitcast.8), custom_call_target="tpu_custom_call" | custom-call | flops 1000000000 | bytes 81920 | tf_op jit(solution)/shard_map/pallas_call | solution.py:194
  26.3 18.6 %all_to_all.16 = f32[32,9,1,128]{3,2,1,0:T(1,128)S(1)} all-to-all(f32[32,9,1,128]{3,2,1,0:T(1,128)S(1)} %bitcast.7), channel_id=1, replica_groups={{22,1,2,3,4,5,6,7,8,9,10,11,12,13,14,15,16,17,18,19,20,21,0,23,24,25,26..., dimensions={0} | all-to-all | bytes 294912 | tf_op jit(solution)/shard_map/all_to_all | solution.py:210
  44.9 0.8 %shard_map.61 = f32[160,128]{1,0:T(8,128)S(1)} custom-call(f32[4,256,256]{2,1,0:T(8,128)S(1)} %copy-done, f32[16,64]{1,0:T(8,128)S(1)} %copy-done.1, bf16[256,128]{1,0:T(8,128)(2,1)S(1)} %get-tuple-element.4.cc_ref, f32[160,128]{1,0:T(8,128)S(1)} %bitcast.9, f32[288,128]{1,0:T(8,128)S(1)} %bitcast.6), custom_call_target="tpu_custom_call" | custom-call | flops 1000000000 | bytes 81920 | tf_op jit(solution)/shard_map/pallas_call | solution.py:194
  45.7 11.5 %all_to_all.17 = f32[32,5,1,128]{3,2,1,0:T(1,128)S(1)} all-to-all(f32[32,5,1,128]{3,2,1,0:T(1,128)S(1)} %bitcast.10), channel_id=1, replica_groups={{384,32,64,96,128,160,192,224,256,288,320,352,0,416,448,480,512,544,576..., dimensions={0} | all-to-all | bytes 163840 | tf_op jit(solution)/shard_map/all_to_all | solution.py:210
  57.3 0.7 %shard_map.62 = (f32[2,64]{1,0:T(2,128)}, f32[8,64]{1,0:T(8,128)}) custom-call(f32[160,128]{1,0:T(8,128)S(1)} %bitcast.11), custom_call_target="tpu_custom_call" | custom-call | flops 1000000000 | bytes 81920 | tf_op jit(solution)/shard_map/pallas_call | solution.py:194
Async XLA Ops:
  0.6 25.0 %copy-start = (f32[4,256,256]{2,1,0:T(8,128)S(1)}, f32[4,256,256]{2,1,0:T(8,128)}, u32[]{:S(2)}) copy-start(f32[4,256,256]{2,1,0:T(8,128)} %t_ref.3) | copy-start | bytes 3145732
  1.5 24.1 %copy-start.1 = (f32[16,64]{1,0:T(8,128)S(1)}, f32[16,64]{1,0:T(8,128)}, u32[]{:S(2)}) copy-start(f32[16,64]{1,0:T(8,128)} %a_ref.3) | copy-start | bytes 12292

commit v9 on v6

--- a/solution.py
+++ b/solution.py
@@ -151,7 +151,7 @@
         t_hi, t_lo = split(t_ref[i])
         part = dot(x, t_hi) + dot(x, t_lo)
         third = part if third is None else third + part
-    gram_b = dot(jnp.concatenate(split(bt), axis=0), parts(b))
+    gram_b = dot(parts(b), parts(b), ((0,), (0,)))
     gram_b = twice(gram_b[:R, :] + gram_b[R:, :])
     gram_a = a_turned[:, 0:1] * aa[0:1, :]
     for i in range(1, NI):

time: 58.2 us -> 58.2 us (level)
  no operation moved by 1% of the time
where the time goes in v9:
time: 58.2 us; the launch traced here: 57.9 us
  blocking collectives  54.2 us (93%)
  Pallas kernels  3.06 us (5%)
  between operations  0.66 us (1%)
    all_to_all x3, blocking collectives, exchange(): x = lax.all_to_all(x, axes, 0, 0, axis_index_groups=[order])  54.2 us
    pallas_call x3, Pallas kernels, call(): pl.pallas_call(kernel, out_shape=[jax.ShapeDtypeStruct(shape, kind) for s...  2.17 us

profile of v9, /device:TPU:1, one launch (start us, length us, event | category | flops | bytes accessed | tf_op | source)
XLA Modules:
  0.0 57.9 jit_solution(3094026876641243973)
XLA Ops:
  0.6 0.0 copy-start
  0.6 0.9 %shard_map.59 = f32[160,128]{1,0:T(8,128)S(1)} custom-call(f32[2,64]{1,0:T(2,128)} %b_hbm.1, f32[8,64]{1,0:T(8,128)} %c_hbm.1), custom_call_target="tpu_custom_call" | custom-call | flops 1000000000 | bytes 81920 | tf_op jit(solution)/shard_map/pallas_call | solution.py:215
  1.5 0.0 copy-start.1
  1.5 24.1 %all_to_all.15 = f32[32,5,1,128]{3,2,1,0:T(1,128)S(1)} all-to-all(f32[32,5,1,128]{3,2,1,0:T(1,128)S(1)} %bitcast.12), channel_id=1, replica_groups={{384,32,64,96,128,160,192,224,256,288,320,352,0,416,448,480,512,544,576..., dimensions={0} | all-to-all | bytes 163840 | tf_op jit(solution)/shard_map/all_to_all | solution.py:210
  25.6 0.0 copy-done
  25.6 0.0 copy-done.1
  25.6 0.7 %shard_map.60 = (f32[288,128]{1,0:T(8,128)S(1)}, bf16[256,128]{1,0:T(8,128)(2,1)S(1)}) custom-call(f32[4,256,256]{2,1,0:T(8,128)S(1)} %copy-done, f32[16,64]{1,0:T(8,128)S(1)} %copy-done.1, f32[160,128]{1,0:T(8,128)S(1)} %bitcast.8), custom_call_target="tpu_custom_call" | custom-call | flops 1000000000 | bytes 81920 | tf_op jit(solution)/shard_map/pallas_call | solution.py:194
  26.3 17.6 %all_to_all.16 = f32[32,9,1,128]{3,2,1,0:T(1,128)S(1)} all-to-all(f32[32,9,1,128]{3,2,1,0:T(1,128)S(1)} %bitcast.7), channel_id=1, replica_groups={{26,1,2,3,4,5,6,7,8,9,10,11,12,13,14,15,16,17,18,19,20,21,22,23,24,25,0..., dimensions={0} | all-to-all | bytes 294912 | tf_op jit(solution)/shard_map/all_to_all | solution.py:210
  43.9 0.8 %shard_map.61 = f32[160,128]{1,0:T(8,128)S(1)} custom-call(f32[4,256,256]{2,1,0:T(8,128)S(1)} %copy-done, f32[16,64]{1,0:T(8,128)S(1)} %copy-done.1, bf16[256,128]{1,0:T(8,128)(2,1)S(1)} %get-tuple-element.4.cc_ref, f32[160,128]{1,0:T(8,128)S(1)} %bitcast.9, f32[288,128]{1,0:T(8,128)S(1)} %bitcast.6), custom_call_target="tpu_custom_call" | custom-call | flops 1000000000 | bytes 81920 | tf_op jit(solution)/shard_map/pallas_call | solution.py:194
  44.7 12.5 %all_to_all.17 = f32[32,5,1,128]{3,2,1,0:T(1,128)S(1)} all-to-all(f32[32,5,1,128]{3,2,1,0:T(1,128)S(1)} %bitcast.10), channel_id=1, replica_groups={{384,32,64,96,128,160,192,224,256,288,320,352,0,416,448,480,512,544,576..., dimensions={0} | all-to-all | bytes 163840 | tf_op jit(solution)/shard_map/all_to_all | solution.py:210
  57.2 0.7 %shard_map.62 = (f32[2,64]{1,0:T(2,128)}, f32[8,64]{1,0:T(8,128)}) custom-call(f32[160,128]{1,0:T(8,128)S(1)} %bitcast.11), custom_call_target="tpu_custom_call" | custom-call | flops 1000000000 | bytes 81920 | tf_op jit(solution)/shard_map/pallas_call | solution.py:194
Async XLA Ops:
  0.6 25.0 %copy-start = (f32[4,256,256]{2,1,0:T(8,128)S(1)}, f32[4,256,256]{2,1,0:T(8,128)}, u32[]{:S(2)}) copy-start(f32[4,256,256]{2,1,0:T(8,128)} %t_ref.3) | copy-start | bytes 3145732
  1.5 24.1 %copy-start.1 = (f32[16,64]{1,0:T(8,128)S(1)}, f32[16,64]{1,0:T(8,128)}, u32[]{:S(2)}) copy-start(f32[16,64]{1,0:T(8,128)} %a_ref.3) | copy-start | bytes 12292
